TPU v7x, 256 devices: a whole 4x4x8 slice. The times are simulated.
256 devices in a mesh: dom: 256 (over z, x, y, core).
Axes of the slice: x: 4, y: 4, z: 8, core: 2. Of those that a mesh axis runs over, the one named last changes fastest.
Arguments:
- coef_init: float32 [1024, 128], P('dom'), may hold values from -6 to 6
- basis: bfloat16 [393216, 1024], P('dom'), may hold values from -0.75 to 0.75
- basis_scale: float32 [3072], P('dom'), may hold values from 0.5 to 2
- ext_force: float32 [393216, 128], P('dom'), may hold values from -6 to 6
- precond: float32 [1024], P('dom'), may hold values from 0.5 to 6, as said below
- connectivity: int32 [115200, 8], P('dom'), may hold values from 0 to 767, as said below
- halo_nodes: int32 [65536], P('dom'), may hold values from 0 to 511, as said below
- plastic: int32 [115200], P('dom'), may hold values 0 or 1
Outputs:
- coef_final: float32 [1024, 128], P('dom')
- nodal_residual: float32 [393216, 128], P('dom')
Inputs may be any that keep to these rules, and one draw needn't show every extreme that they name: `connectivity`: each part is a structured block of 16 x 16 x 2 nodes, numbered in a part-specific order; each row lists an element's 8 corners in corner-bit order (bit 0 along x, bit 1 along y, bit 2 along z). Entries below 512 are the part's own nodes; an entry 512 + h names the node listed h-th in the next part's halo_nodes (the next part's first z layer). `halo_nodes`: the entries of one part are its own local node numbers of its first z layer, in grid order with x fastest, all distinct. `precond`: Positive.
All inputs are finite; a program needn't handle non-finite values. No bound on the sum of `plastic` on one device may be relied on, other than what follows from the above.
Results may differ from a plain program's by a relative error of at most 0.0087.
Values may be sent and summed in bfloat16 or wider, within the bound.
A program may use at most 64 MiB of HBM per device.

v0:
```python
import jax
import jax.numpy as jnp
from jax import lax
from jax.sharding import PartitionSpec as P

R = 1024
ITERS = 2
STEP_SIZE = 0.5
SHEAR_MODULUS = 1.0
LAME_FIRST = 1.5
HARDENING = 0.5
YIELD_STRESS = 3.0
EPSILON = 1e-05


def from_behind(value, axis, steps):
    count = lax.axis_size(axis)
    leading, last = (max(0, -steps), min(count, count - steps))
    return lax.ppermute(value, axis, [(source, source + steps) for source in range(leading, last)])


def corner_table():
    corner_bits = jnp.arange(8)[:, None] >> jnp.arange(3)[None, :] & 1
    return (2.0 * corner_bits.astype(jnp.float32) - 1.0) / 4.0


def element_forces(corner_disp, flags, corners):
    gradient = jnp.einsum("eaic,aj->eijc", corner_disp, corners, precision=lax.Precision.HIGHEST)
    strain = 0.5 * (gradient + jnp.swapaxes(gradient, 1, 2))
    volumetric = strain[:, 0, 0] + strain[:, 1, 1] + strain[:, 2, 2]
    identity = jnp.eye(3, dtype=jnp.float32)[None, :, :, None]
    shear_part = 2.0 * SHEAR_MODULUS * (strain - volumetric[:, None, None] / 3.0 * identity)
    magnitude = jnp.sqrt(jnp.sum(shear_part * shear_part, axis=(1, 2)))
    total_modulus = 2.0 * SHEAR_MODULUS + HARDENING
    plastic_factor = HARDENING / total_modulus + 2.0 * SHEAR_MODULUS * YIELD_STRESS / (
        total_modulus * jnp.maximum(magnitude, YIELD_STRESS)
    )
    factor = jnp.where(flags[:, None] == 1, plastic_factor, jnp.ones_like(plastic_factor))
    stress = LAME_FIRST * volumetric[:, None, None] * identity + factor[:, None, None] * shear_part
    return jnp.einsum("eijc,aj->eaic", stress, corners, precision=lax.Precision.HIGHEST)


def apply_scale(values, scales):
    return (values.reshape(scales.shape[0], -1, values.shape[-1]) * scales[:, None, None]).reshape(
        values.shape
    )


def on_device(coef_init, basis, basis_scale, ext_force, precond, connectivity, halo_nodes, plastic):
    rows_dev, cases = ext_force.shape
    node_count = rows_dev // 3
    halo_count = halo_nodes.shape[0]
    corners = corner_table()
    node_ids = jnp.arange(node_count + halo_count, dtype=jnp.int32)
    incidence = (node_ids[:, None] == connectivity.reshape(-1)[None, :]).astype(jnp.float32)
    nodal_residual = ext_force
    coef_out = coef_init
    for sweep in range(ITERS):
        lifted = jnp.dot(
            basis,
            lax.all_gather(coef_out.astype(jnp.bfloat16), "dom", axis=0, tiled=True),
            preferred_element_type=jnp.float32,
        )
        nodes = apply_scale(lifted, basis_scale).reshape(node_count, 3, cases)
        outgoing = nodes[halo_nodes]
        residual_incoming = from_behind(outgoing, "dom", -1)
        extended = jnp.concatenate([nodes, residual_incoming], axis=0)
        corner_force = element_forces(extended[connectivity], plastic, corners)
        internal = jnp.dot(
            incidence,
            corner_force.reshape(-1, 3 * cases),
            precision=lax.Precision.HIGHEST,
            preferred_element_type=jnp.float32,
        ).reshape(node_count + halo_count, 3, cases)
        returned = from_behind(internal[node_count:], "dom", 1)
        own_force = internal[:node_count].at[halo_nodes].add(returned)
        nodal_residual = ext_force - own_force.reshape(rows_dev, cases)
        scaled = apply_scale(nodal_residual, basis_scale).astype(jnp.bfloat16)
        reduced = lax.psum_scatter(
            lax.dot_general(
                basis, scaled, (((0,), (0,)), ((), ())), preferred_element_type=jnp.float32
            ),
            "dom",
            scatter_dimension=0,
            tiled=True,
        )
        update = precond[:, None] * reduced
        squares = lax.psum(jnp.sum(update * update, axis=0), "dom")
        root_mean = jnp.sqrt(squares / R + EPSILON)
        coef_out = coef_out + STEP_SIZE * update / root_mean
    return (coef_out, nodal_residual)


def solution(mesh):
    return jax.shard_map(
        on_device,
        mesh=mesh,
        in_specs=(
            P("dom", None),
            P("dom", None),
            P("dom"),
            P("dom", None),
            P("dom"),
            P("dom", None),
            P("dom"),
            P("dom"),
        ),
        out_specs=(P("dom", None), P("dom", None)),
        check_vma=False,
    )
```

profile of v0, /device:TPU:1, one launch (start us, length us, event | category | flops | bytes accessed | tf_op | source)
XLA Modules:
  0.0 1042.2 jit_solution(15831920046400500216)
XLA Ops:
  9.8 67.0 %all-gather = bf16[256,4,128]{2,1,0:T(4,128)(2,1)S(1)} all-gather(bf16[1,4,128]{2,1,0:T(4,128)(2,1)S(1)} %convert_bitcast_fusion.1), channel_id=1, replica_groups=mesh['dom'=256] {'dom'}, dimensions={0}, use_global_device_ids=true | all-gather | bytes 263168 | tf_op jit(solution)/shard_map/all_gather | solution.py:61
  76.8 1.9 fusion.51
  78.7 2.3 reshape.92
  81.0 2.8 broadcast_multiply_fusion.1
  83.8 3.0 gather_fusion
  86.8 2.1 collective-permute-start
  92.8 4.8 collective-permute-done
  97.6 3.0 pad_maximum_fusion
  100.6 14.1 %gather_fusion.1 = f32[3600,3,128]{2,1,0:T(4,128)} fusion(f32[768,3,128]{2,1,0:T(4,128)} %pad_maximum_fusion, s32[4096]{0:T(1024)S(1)} %pad_clamp_fusion), kind=kCustom, calls=%fused_computation.1 | custom fusion | bytes 11073600 | tf_op jit(solution)/shard_map/gather | solution.py:68
  114.7 8.2 fusion.6
  124.9 2.2 multiply_reduce_fusion.1
  127.3 4.6 multiply_add_fusion.1
  131.9 6.6 convolution_bitcast_fusion.1
  138.4 8.3 fusion.1
  148.6 2.0 copy.43
  150.5 1.9 collective-permute-start.1
  152.5 2.1 slice.67
  154.6 2.5 copy.44
  157.1 1.8 collective-permute-done.1
  158.9 26.5 %scatter_fusion = f32[512,3,128]{2,1,0:T(4,128)} fusion(f32[512,3,128]{2,1,0:T(4,128)} %copy.44, s32[256]{0:T(256)S(1)} %compare_select_fusion.1, f32[256,3,128]{2,1,0:T(4,128)} %collective-permute-done.1), kind=kCustom, calls=%fused_computation.4 | custom fusion | flops 98304 | bytes 1180672 | tf_op jit(solution)/shard_map/scatter-add | solution.py:76
  185.4 2.3 reshape.94
  187.7 3.2 convolution_bitcast_fusion.4
  191.1 253.2 %all-reduce.5.cloned.1.call-done = f32[1024,128]{0,1:T(8,128)} async-done(((f32[1024,128]{0,1:T(8,128)}), f32[1024,128]{0,1:T(8,128)}) %all-reduce.5.cloned.1.call-update) | async-done | bytes 524304
  445.4 77.5 %psum.14 = f32[128]{0:T(128)S(1)} all-reduce(f32[128]{0:T(128)S(1)} %multiply_reduce_fusion.3), channel_id=1, replica_groups=mesh['dom'=256] {'dom'}, use_global_device_ids=true, to_apply=%region_4.5 | all-reduce | flops 128 | bytes 1024 | tf_op jit(solution)/shard_map/psum | solution.py:88
  524.4 58.8 %all-gather.1 = bf16[256,4,128]{2,1,0:T(4,128)(2,1)S(1)} all-gather(bf16[1,4,128]{2,1,0:T(4,128)(2,1)S(1)} %copy.46), channel_id=1, replica_groups=mesh['dom'=256] {'dom'}, dimensions={0}, use_global_device_ids=true | all-gather | bytes 263168 | tf_op jit(solution)/shard_map/all_gather | solution.py:61
  583.3 2.1 convolution_bitcast_fusion.2
  585.3 2.3 copy.47
  587.7 2.3 reshape.95
  590.0 2.8 broadcast_multiply_fusion
  592.8 3.0 gather_fusion.2
  595.8 2.1 collective-permute-start.2
  597.8 8.7 collective-permute-done.2
  606.6 2.8 pad_maximum_fusion.1
  609.4 14.1 %gather_fusion.3 = f32[3600,3,128]{2,1,0:T(4,128)} fusion(f32[768,3,128]{2,1,0:T(4,128)} %pad_maximum_fusion.1, s32[4096]{0:T(1024)S(1)} %pad_clamp_fusion), kind=kCustom, calls=%fused_computation.3 | custom fusion | bytes 11073600 | tf_op jit(solution)/shard_map/gather | solution.py:68
  623.5 8.2 fusion.4
  633.6 2.2 multiply_reduce_fusion
  636.0 4.6 multiply_add_fusion
  640.6 6.6 convolution_bitcast_fusion
  647.2 8.3 fusion
  657.5 1.9 collective-permute-start.3
  659.5 2.1 slice.72
  661.5 2.5 copy.53
  664.0 1.9 collective-permute-done.3
  665.9 26.5 %scatter_fusion.1 = f32[512,3,128]{2,1,0:T(4,128)} fusion(f32[512,3,128]{2,1,0:T(4,128)} %copy.53, s32[256]{0:T(256)S(1)} %compare_select_fusion.1, f32[256,3,128]{2,1,0:T(4,128)} %collective-permute-done.3), kind=kCustom, calls=%fused_computation.5 | custom fusion | flops 98304 | bytes 1180672 | tf_op jit(solution)/shard_map/scatter-add | solution.py:76
  692.4 2.3 reshape.97
  697.0 1.8 convolution_bitcast_fusion.3
  698.9 256.0 %all-reduce.7.cloned.1.call-done = f32[1024,128]{0,1:T(8,128)} async-done(((f32[1024,128]{0,1:T(8,128)}), f32[1024,128]{0,1:T(8,128)}) %all-reduce.7.cloned.1.call-update) | async-done | bytes 524304
  955.9 77.5 %psum.15 = f32[128]{0:T(128)S(1)} all-reduce(f32[128]{0:T(128)S(1)} %multiply_reduce_fusion.2), channel_id=1, replica_groups=mesh['dom'=256] {'dom'}, use_global_device_ids=true, to_apply=%region_9.10 | all-reduce | flops 128 | bytes 1024 | tf_op jit(solution)/shard_map/psum | solution.py:88
  (72 shorter events, 22.2 us)
Async XLA Ops:
  7.2 69.6 %copy-start = (bf16[1536,1024]{1,0:T(8,128)(2,1)S(1)}, bf16[1536,1024]{1,0:T(8,128)(2,1)}, u32[]{:S(2)}) copy-start(bf16[1536,1024]{1,0:T(8,128)(2,1)} %param.9) | copy-start | bytes 9437188
  7.2 437.2 %all-reduce.5.cloned.1.call-start = ((), (), s32[]{:S(2)}) async-start(), calls=%async_computation | async-start | bytes 1048576
  78.7 10.2 copy-start.6
  78.7 14.1 %copy-start.14 = (s32[450]{0:T(512)S(1)}, s32[450]{0:T(512)}, u32[]{:S(2)}) copy-start(s32[450]{0:T(512)} %param.15) | copy-start | bytes 5404
  86.8 10.8 %collective-permute-start = (f32[256,3,128]{2,1,0:T(4,128)}, f32[256,3,128]{2,1,0:T(4,128)}, u32[]{:S(2)}, u32[]{:S(2)}) collective-permute-start(f32[256,3,128]{2,1,0:T(4,128)} %gather_fusion), channel_id=1, source_target_pairs={{1,0},{2,1},{3,2},{4,3},{5,4},{6,5},{7,6},{8,7},{9,8},{10,9},{11,1... | collective-permute-start | bytes 1179656 | tf_op jit(solution)/shard_map/ppermute | solution.py:19
  92.7 45.7 %copy-start.7 = (s32[3600]{0:T(1024)}, s32[3600]{0:T(1024)S(1)}, u32[]{:S(2)}) copy-start(s32[3600]{0:T(1024)S(1)} %eq.35) | copy-start | bytes 43204
  138.4 14.0 %copy-start.13 = (f32[12]{0:T(128)S(1)}, f32[12]{0:T(128)}, u32[]{:S(2)}) copy-start(f32[12]{0:T(128)} %param.10) | copy-start | bytes 148
  146.8 1.0 copy-start.2
  150.5 8.3 collective-permute-start.1
  187.7 3.3 copy-start.10
  187.7 256.6 %copy-start.9 = (f32[4]{0:T(128)S(1)}, f32[4]{0:T(128)}, u32[]{:S(2)}) copy-start(f32[4]{0:T(128)} %param.12) | copy-start | bytes 52
  190.9 764.0 %all-reduce.7.cloned.1.call-start = ((), (), s32[]{:S(2)}) async-start(), calls=%async_computation.1 | async-start | bytes 1048576
  191.1 396.6 %copy-start.4 = (f32[4,128]{0,1:T(8,128)}, f32[4,128]{0,1:T(8,128)S(1)}, u32[]{:S(2)}) copy-start(f32[4,128]{0,1:T(8,128)S(1)} %copy.45) | copy-start | bytes 6148
  522.9 0.5 copy-start.11
  595.8 10.8 %collective-permute-start.2 = (f32[256,3,128]{2,1,0:T(4,128)}, f32[256,3,128]{2,1,0:T(4,128)S(1)}, u32[]{:S(2)}, u32[]{:S(2)}) collective-permute-start(f32[256,3,128]{2,1,0:T(4,128)} %gather_fusion.2), channel_id=1, source_target_pairs={{1,0},{2,1},{3,2},{4,3},{5,4},{6,5},{7,6},{8,7},{9,8},{10,9},{11,1... | collective-permute-start | bytes 1179656 | tf_op jit(solution)/shard_map/ppermute | solution.py:19
  640.6 6.6 copy-start.8
  655.5 1.0 copy-start.3
  657.5 8.3 collective-permute-start.3
  696.1 0.9 copy-start.1
  697.0 336.4 %copy-start.5 = (f32[4,128]{0,1:T(8,128)S(1)}, f32[4,128]{0,1:T(8,128)}, u32[]{:S(2)}) copy-start(f32[4,128]{0,1:T(8,128)} %copy-done.4) | copy-start | bytes 6148
  697.0 336.4 %copy-start.12 = (f32[128]{0:T(128)S(1)}, f32[128]{0:T(128)}, u32[]{:S(2)}) copy-start(f32[128]{0:T(128)} %copy-done.11) | copy-start | bytes 1540
Sparse Core Ops, SparseCore 0:
  191.0 253.2 all-reduce.4
  699.0 255.8 all-reduce.6
where the time goes:
time: 1050 us; the launch traced here: 1040 us
  waiting for transfers between devices  527 us (50%)
  blocking collectives  281 us (27%)
  other arithmetic  89.2 us (8%)
  local copies, waits for them, and re-layouts  67.7 us (6%)
  matrix products  55 us (5%)
  between operations  14.7 us (1%)
    unnamed x4, waiting for transfers between devices  509 us
    psum x2, blocking collectives, on_device(): squares = lax.psum(jnp.sum(update * update, axis=0), 'dom')  155 us
    all_gather x2, blocking collectives, on_device(): lax.all_gather(coef_out.astype(jnp.bfloat16), 'dom', axis=0, tiled=True)  126 us
    scatter-add x2, other arithmetic, on_device(): own_force = internal[:node_count].at[halo_nodes].add(returned)  53.1 us
    gather x2, local copies, waits for them, and re-layouts, on_device(): corner_force = element_forces(extended[connectivity], plastic, corners)  28.2 us
  transfers between devices with their start and end apart: 6, of which 6 were waited for; matrix products, arithmetic and copies ran while one was open for 1% of the time, Pallas kernels for 0%

commit v1 on v0

--- a/solution.py
+++ b/solution.py
@@ -85,7 +85,7 @@
             tiled=True,
         )
         update = precond[:, None] * reduced
-        squares = lax.psum(jnp.sum(update * update, axis=0), "dom")
+        squares = jnp.sum(lax.all_gather(jnp.sum(update * update, axis=0), "dom"), axis=0)
         root_mean = jnp.sqrt(squares / R + EPSILON)
         coef_out = coef_out + STEP_SIZE * update / root_mean
     return (coef_out, nodal_residual)

time: 1050 us -> 1020 us (0.971)
  blocking collectives: 281 us -> 245 us
    psum x2 -> x0, blocking collectives: 155 us -> none  [on_device(): squares = lax.psum(jnp.sum(update * update, axis=0), 'dom')]
    all_gather x0 -> x2, blocking collectives: none -> 118 us  [on_device(): lax.all_gather(jnp.sum(update * update, axis=0), 'dom')]
where the time goes in v1:
time: 1020 us; the launch traced here: 1010 us
  waiting for transfers between devices  525 us (51%)
  blocking collectives  245 us (24%)
  other arithmetic  90.7 us (9%)
  local copies, waits for them, and re-layouts  67.7 us (7%)
  matrix products  55 us (5%)
  between operations  14.7 us (1%)
    unnamed x4, waiting for transfers between devices  507 us
    all_gather x2, blocking collectives, on_device(): lax.all_gather(coef_out.astype(jnp.bfloat16), 'dom', axis=0, tiled=True)  126 us
    all_gather x2, blocking collectives, on_device(): lax.all_gather(jnp.sum(update * update, axis=0), 'dom')  118 us
    scatter-add x2, other arithmetic, on_device(): own_force = internal[:node_count].at[halo_nodes].add(returned)  53.1 us
    gather x2, local copies, waits for them, and re-layouts, on_device(): corner_force = element_forces(extended[connectivity], plastic, corners)  28.2 us
  transfers between devices with their start and end apart: 6, of which 6 were waited for; matrix products, arithmetic and copies ran while one was open for 1% of the time, Pallas kernels for 0%

profile of v1, /device:TPU:1, one launch (start us, length us, event | category | flops | bytes accessed | tf_op | source)
XLA Modules:
  0.0 1005.5 jit_solution(9858153377836680898)
XLA Ops:
  9.8 67.0 %all-gather.2 = bf16[256,4,128]{2,1,0:T(4,128)(2,1)S(1)} all-gather(bf16[1,4,128]{2,1,0:T(4,128)(2,1)S(1)} %convert_bitcast_fusion.1), channel_id=1, replica_groups=mesh['dom'=256] {'dom'}, dimensions={0}, use_global_device_ids=true | all-gather | bytes 263168 | tf_op jit(solution)/shard_map/all_gather | solution.py:61
  76.8 1.9 fusion.51
  78.7 2.3 reshape.100
  81.0 2.8 broadcast_multiply_fusion.1
  83.8 3.0 gather_fusion
  86.8 2.1 collective-permute-start
  92.8 4.8 collective-permute-done
  97.6 3.0 pad_maximum_fusion
  100.6 14.1 %gather_fusion.1 = f32[3600,3,128]{2,1,0:T(4,128)} fusion(f32[768,3,128]{2,1,0:T(4,128)} %pad_maximum_fusion, s32[4096]{0:T(1024)S(1)} %pad_clamp_fusion), kind=kCustom, calls=%fused_computation.1 | custom fusion | bytes 11073600 | tf_op jit(solution)/shard_map/gather | solution.py:68
  114.7 8.2 fusion.6
  124.9 2.2 multiply_reduce_fusion.1
  127.3 4.6 multiply_add_fusion.1
  131.9 6.6 convolution_bitcast_fusion.1
  138.4 8.3 fusion.1
  148.6 2.0 copy.43
  150.5 1.9 collective-permute-start.1
  152.5 2.1 slice.67
  154.6 2.5 copy.44
  157.1 1.8 collective-permute-done.1
  158.9 26.5 %scatter_fusion = f32[512,3,128]{2,1,0:T(4,128)} fusion(f32[512,3,128]{2,1,0:T(4,128)} %copy.44, s32[256]{0:T(256)S(1)} %compare_select_fusion.1, f32[256,3,128]{2,1,0:T(4,128)} %collective-permute-done.1), kind=kCustom, calls=%fused_computation.4 | custom fusion | flops 98304 | bytes 1180672 | tf_op jit(solution)/shard_map/scatter-add | solution.py:76
  185.4 2.3 reshape.102
  187.7 3.2 convolution_bitcast_fusion.4
  191.1 253.2 %all-reduce.5.cloned.1.call-done = f32[1024,128]{0,1:T(8,128)} async-done(((f32[1024,128]{0,1:T(8,128)}), f32[1024,128]{0,1:T(8,128)}) %all-reduce.5.cloned.1.call-update) | async-done | bytes 524304
  445.4 61.0 %all-gather.3 = f32[256,1,128]{2,1,0:T(1,128)} all-gather(f32[1,1,128]{2,1,0:T(1,128)S(1)} %bitcast.102), channel_id=2, replica_groups=mesh['dom'=256] {'dom'}, dimensions={0}, use_global_device_ids=true | all-gather | bytes 131584 | tf_op jit(solution)/shard_map/all_gather | solution.py:88
  509.1 59.2 %all-gather.4 = bf16[256,4,128]{2,1,0:T(4,128)(2,1)S(1)} all-gather(bf16[1,4,128]{2,1,0:T(4,128)(2,1)S(1)} %copy.46), channel_id=1, replica_groups=mesh['dom'=256] {'dom'}, dimensions={0}, use_global_device_ids=true | all-gather | bytes 263168 | tf_op jit(solution)/shard_map/all_gather | solution.py:61
  568.3 2.1 convolution_bitcast_fusion.2
  570.3 2.3 copy.47
  572.7 2.3 reshape.103
  575.0 2.8 broadcast_multiply_fusion
  577.8 3.0 gather_fusion.2
  580.8 2.1 collective-permute-start.2
  582.9 8.6 collective-permute-done.2
  591.5 2.8 pad_maximum_fusion.1
  594.3 14.1 %gather_fusion.3 = f32[3600,3,128]{2,1,0:T(4,128)} fusion(f32[768,3,128]{2,1,0:T(4,128)} %pad_maximum_fusion.1, s32[4096]{0:T(1024)S(1)} %pad_clamp_fusion), kind=kCustom, calls=%fused_computation.3 | custom fusion | bytes 11073600 | tf_op jit(solution)/shard_map/gather | solution.py:68
  608.4 8.2 fusion.4
  618.5 2.2 multiply_reduce_fusion
  620.9 4.6 multiply_add_fusion
  625.5 6.6 convolution_bitcast_fusion
  632.1 8.3 fusion
  642.5 1.9 collective-permute-start.3
  644.4 2.1 slice.72
  646.4 2.5 copy.53
  648.9 1.9 collective-permute-done.3
  650.8 26.5 %scatter_fusion.1 = f32[512,3,128]{2,1,0:T(4,128)} fusion(f32[512,3,128]{2,1,0:T(4,128)} %copy.53, s32[256]{0:T(256)S(1)} %compare_select_fusion.1, f32[256,3,128]{2,1,0:T(4,128)} %collective-permute-done.3), kind=kCustom, calls=%fused_computation.5 | custom fusion | flops 98304 | bytes 1180672 | tf_op jit(solution)/shard_map/scatter-add | solution.py:76
  677.3 2.3 reshape.105
  682.0 1.8 convolution_bitcast_fusion.3
  683.8 254.1 %all-reduce.7.cloned.1.call-done = f32[1024,128]{0,1:T(8,128)} async-done(((f32[1024,128]{0,1:T(8,128)}), f32[1024,128]{0,1:T(8,128)}) %all-reduce.7.cloned.1.call-update) | async-done | bytes 524304
  938.9 57.5 %all-gather.5 = f32[256,1,128]{2,1,0:T(1,128)S(1)} all-gather(f32[1,1,128]{2,1,0:T(1,128)S(1)} %bitcast.103), channel_id=3, replica_groups=mesh['dom'=256] {'dom'}, dimensions={0}, use_global_device_ids=true | all-gather | bytes 131584 | tf_op jit(solution)/shard_map/all_gather | solution.py:88
  (74 shorter events, 23.7 us)
Async XLA Ops:
  7.2 69.6 %copy-start = (bf16[1536,1024]{1,0:T(8,128)(2,1)S(1)}, bf16[1536,1024]{1,0:T(8,128)(2,1)}, u32[]{:S(2)}) copy-start(bf16[1536,1024]{1,0:T(8,128)(2,1)} %param.9) | copy-start | bytes 9437188
  7.2 437.2 %all-reduce.5.cloned.1.call-start = ((), (), s32[]{:S(2)}) async-start(), calls=%async_computation | async-start | bytes 1048576
  78.7 10.2 %copy-start.6 = (s32[450,8]{0,1:T(8,128)S(1)}, s32[450,8]{0,1:T(8,128)}, u32[]{:S(2)}) copy-start(s32[450,8]{0,1:T(8,128)} %param.13) | copy-start | bytes 43204
  78.7 14.1 %copy-start.14 = (s32[450]{0:T(512)S(1)}, s32[450]{0:T(512)}, u32[]{:S(2)}) copy-start(s32[450]{0:T(512)} %param.15) | copy-start | bytes 5404
  86.8 10.8 %collective-permute-start = (f32[256,3,128]{2,1,0:T(4,128)}, f32[256,3,128]{2,1,0:T(4,128)}, u32[]{:S(2)}, u32[]{:S(2)}) collective-permute-start(f32[256,3,128]{2,1,0:T(4,128)} %gather_fusion), channel_id=1, source_target_pairs={{1,0},{2,1},{3,2},{4,3},{5,4},{6,5},{7,6},{8,7},{9,8},{10,9},{11,1... | collective-permute-start | bytes 1179656 | tf_op jit(solution)/shard_map/ppermute | solution.py:19
  92.7 45.7 %copy-start.7 = (s32[3600]{0:T(1024)}, s32[3600]{0:T(1024)S(1)}, u32[]{:S(2)}) copy-start(s32[3600]{0:T(1024)S(1)} %eq.35) | copy-start | bytes 43204
  138.4 14.0 %copy-start.13 = (f32[12]{0:T(128)S(1)}, f32[12]{0:T(128)}, u32[]{:S(2)}) copy-start(f32[12]{0:T(128)} %param.10) | copy-start | bytes 148
  146.8 1.0 copy-start.2
  150.5 8.3 collective-permute-start.1
  187.7 3.3 copy-start.10
  187.7 256.6 %copy-start.9 = (f32[4]{0:T(128)S(1)}, f32[4]{0:T(128)}, u32[]{:S(2)}) copy-start(f32[4]{0:T(128)} %param.12) | copy-start | bytes 52
  190.9 747.0 %all-reduce.7.cloned.1.call-start = ((), (), s32[]{:S(2)}) async-start(), calls=%async_computation.1 | async-start | bytes 1048576
  191.1 381.6 %copy-start.4 = (f32[4,128]{0,1:T(8,128)}, f32[4,128]{0,1:T(8,128)S(1)}, u32[]{:S(2)}) copy-start(f32[4,128]{0,1:T(8,128)S(1)} %copy.45) | copy-start | bytes 6148
  507.5 0.5 copy-start.11
  580.8 10.7 %collective-permute-start.2 = (f32[256,3,128]{2,1,0:T(4,128)}, f32[256,3,128]{2,1,0:T(4,128)S(1)}, u32[]{:S(2)}, u32[]{:S(2)}) collective-permute-start(f32[256,3,128]{2,1,0:T(4,128)} %gather_fusion.2), channel_id=1, source_target_pairs={{1,0},{2,1},{3,2},{4,3},{5,4},{6,5},{7,6},{8,7},{9,8},{10,9},{11,1... | collective-permute-start | bytes 1179656 | tf_op jit(solution)/shard_map/ppermute | solution.py:19
  625.5 6.6 copy-start.8
  640.4 1.0 copy-start.3
  642.5 8.3 collective-permute-start.3
  681.1 0.9 copy-start.1
  681.9 314.8 %copy-start.5 = (f32[4,128]{0,1:T(8,128)S(1)}, f32[4,128]{0,1:T(8,128)}, u32[]{:S(2)}) copy-start(f32[4,128]{0,1:T(8,128)} %copy-done.4) | copy-start | bytes 6148
  681.9 314.8 %copy-start.12 = (f32[128]{0:T(128)S(1)}, f32[128]{0:T(128)}, u32[]{:S(2)}) copy-start(f32[128]{0:T(128)} %copy-done.11) | copy-start | bytes 1540
Sparse Core Ops, SparseCore 0:
  191.0 253.2 all-reduce.4
  683.9 253.9 all-reduce.6
